TPU v7x, 128 devices: a whole 4x4x4 slice. The times are simulated.
128 devices in a mesh: sub: 8 (over z_lo, x), rng: 16 (over z_hi, y, core).
Axes of the slice: x: 4, y: 4, z: 4 (z_hi: 2, z_lo: 2; z = z_hi * 2 + z_lo), core: 2. Of those that a mesh axis runs over, the one named last changes fastest.
Arguments:
- echoes: float32 [2048, 2, 12288], P(('sub', 'rng')), may hold values from -6 to 6
- filter_spectrum: float32 [2, 12288], replicated, may hold values from -3 to 3
- range_shifts: int32 [2048], P('sub'), may hold values from -16 to 16
- steering: bfloat16 [8, 2, 384, 256], P('sub'), may hold values from -0.25 to 0.25
- tap_offsets: int32 [8, 2, 384], P('sub'), may hold values from -3 to 3
- tap_weights: float32 [8, 2, 4, 384], P('sub'), may hold values from -2 to 2
- phase_rates: float32 [8, 2, 384], P('sub'), may hold values from -6 to 6
Outputs:
- tiles: float32 [3072, 2, 12288], P('sub', None, 'rng')
All inputs are finite; a program needn't handle non-finite values.
Results may differ from a plain program's by a relative error of at most 0.0076.
Values may be sent and summed in bfloat16 or wider, within the bound.
A program may use at most 256 MiB of HBM per device.

v0:
```python
import math

import jax
import jax.numpy as jnp
import ml_dtypes
import numpy as np
from jax import lax
from jax.experimental import pallas as pl
from jax.experimental.pallas import tpu as pltpu
from jax.sharding import PartitionSpec as P

RADIX_A = 96
RADIX_B = 128
ANGLES = 384
TAPS = 4
SAMPLES = 12288
SUBS = 8
RANKS = 16
PULSES = 16
PSUB = RANKS * PULSES
BLOCK = SAMPLES // RANKS
ROWS = BLOCK // RADIX_B
CHUNK = BLOCK // SUBS
LEVELS = 3
PARAMS = 16
MESH = pl.DeviceIdType.MESH
F32 = jnp.float32
BF16 = jnp.bfloat16


def halves(table):
    high = table.astype(np.float32).astype(ml_dtypes.bfloat16)
    low = (table - high.astype(np.float64)).astype(np.float32).astype(ml_dtypes.bfloat16)
    return np.stack([high, low])


def tables():
    a = np.arange(RADIX_A)
    b = np.arange(RADIX_B)
    wa = np.exp(-2j * np.pi / RADIX_A * (np.outer(a, a) % RADIX_A))
    wb = np.exp(-2j * np.pi / RADIX_B * (np.outer(b, b) % RADIX_B))
    order = 4 * (b % 32) + b // 32
    wb = wb[:, order]
    vb = np.conj(wb.T)
    va = np.conj(wa)
    left = lambda w: np.block([[w.real, -w.imag], [w.imag, w.real]])
    right = lambda w: np.block([[w.real, w.imag], [-w.imag, w.real]])
    turn = np.exp(-2j * np.pi / SAMPLES * np.outer(a, b))
    twiddle = np.stack([turn.real, turn.imag, turn.real / SAMPLES, -turn.imag / SAMPLES])
    return (
        halves(left(wa)),
        halves(right(wb)),
        halves(right(vb)),
        halves(left(va)),
        twiddle.astype(np.float32),
    )


def split(x):
    high = x.astype(BF16)
    return high, (x - high.astype(F32)).astype(BF16)


def dot(left, right):
    return jnp.dot(left, right, preferred_element_type=F32)


def left_product(table, x):
    high, low = split(x)
    return dot(table[0], high) + dot(table[0], low) + dot(table[1], high)


def right_product(x, table):
    high, low = split(x)
    return dot(high, table[0]) + dot(low, table[0]) + dot(high, table[1])


def times(ar, ai, br, bi):
    return ar * br - ai * bi, ar * bi + ai * br


def compress_kernel(shift_ref, x_ref, f_ref, wa, wb, vb, va, tw, out_ref, filt, rows):
    first = lax.axis_index("rng") * PULSES
    lane32 = lax.broadcasted_iota(jnp.int32, (32, RADIX_B), 1)
    for c in range(2):
        f0, f1, f2 = (f_ref[pl.ds(2 * e + c, 32, stride=6), :] for e in range(3))
        parts = [
            f0,
            jnp.where(lane32 < 32, pltpu.roll(f0, 32, 1), pltpu.roll(f1, 32, 1)),
            jnp.where(lane32 < 64, pltpu.roll(f1, 64, 1), pltpu.roll(f2, 64, 1)),
            pltpu.roll(f2, 96, 1),
        ]
        filt[c] = jnp.concatenate(parts, axis=0).T[:RADIX_A]
    lane = lax.broadcasted_iota(jnp.int32, (RADIX_A, RADIX_B), 1)
    row = lax.broadcasted_iota(jnp.int32, (RADIX_A, RADIX_B), 0)

    def pair(i, carry):
        start = i * 4 * RADIX_A
        signal = jnp.concatenate(
            [
                jnp.concatenate(
                    [x_ref[pl.ds(start + q * 2 * RADIX_A + c, RADIX_A, stride=2), :] for c in range(2)],
                    axis=0,
                )
                for q in range(2)
            ],
            axis=1,
        )
        section = left_product(wa, signal)
        turned = []
        for q in range(2):
            cols = slice(q * RADIX_B, (q + 1) * RADIX_B)
            zr, zi = times(section[:RADIX_A, cols], section[RADIX_A:, cols], tw[0], tw[1])
            turned.append(jnp.concatenate([zr, zi], axis=1))
        spectrum = right_product(jnp.concatenate(turned, axis=0), wb)
        filtered = []
        for q in range(2):
            part = spectrum[q * RADIX_A : (q + 1) * RADIX_A]
            zr, zi = times(part[:, :RADIX_B], part[:, RADIX_B:], filt[0], filt[1])
            filtered.append(jnp.concatenate([zr, zi], axis=1))
        section = right_product(jnp.concatenate(filtered, axis=0), vb)
        turned = []
        for q in range(2):
            part = section[q * RADIX_A : (q + 1) * RADIX_A]
            zr, zi = times(part[:, :RADIX_B], part[:, RADIX_B:], tw[2], tw[3])
            turned.append(jnp.concatenate([zr, zi], axis=0))
        result = left_product(va, jnp.concatenate(turned, axis=1))
        for q in range(2):
            p = 2 * i + q
            shift = shift_ref[first + p]
            step = jnp.where(shift > 0, 1, -1)
            source = lane + shift
            inside = jnp.logical_and(source >= 0, source < RADIX_B)
            next_row = row + step
            present = jnp.logical_and(next_row >= 0, next_row < RADIX_A)
            for c in range(2):
                values = result[c * RADIX_A : (c + 1) * RADIX_A, q * RADIX_B : (q + 1) * RADIX_B]
                turned_lanes = pltpu.roll(values, lax.rem(RADIX_B - shift, RADIX_B), 1)
                beside = pltpu.roll(turned_lanes, lax.rem(RADIX_A - step, RADIX_A), 0)
                moved = jnp.where(inside, turned_lanes, jnp.where(present, beside, 0.0))
                rows[pl.ds(c * RADIX_A * PULSES + p, RADIX_A, stride=PULSES), :] = moved
        return carry

    lax.fori_loop(0, PULSES // 2, pair, 0)

    def pack(j, carry):
        for c in range(2):
            start = pl.multiple_of((c * RADIX_A + j * ROWS) * PULSES, ROWS * PULSES)
            block = rows[pl.ds(start, ROWS * PULSES), :].astype(BF16)
            out_ref[j, c] = block.reshape(ROWS, PULSES, RADIX_B)
        return carry

    lax.fori_loop(0, RANKS, pack, 0)


def partner_of(group, level):
    bit = 1 << level
    return group + bit - 2 * bit * lax.rem(group // bit, 2)


def merge_kernel(
    pulses_ref, steer_ref, off_ref, weight_ref, rate_ref, out_ref,
    held, params, left, steer, band, phase, sent, image, done,
    pulse_send, pulse_recv, param_send, param_recv, image_send, image_recv, tile_send, tile_recv, local_sem,
):
    sub = lax.axis_index("sub")
    rng = lax.axis_index("rng")
    barrier = pltpu.get_barrier_semaphore()
    for k in range(1, RANKS):
        pl.semaphore_signal(barrier, inc=1, device_id={"rng": lax.rem(rng + k, RANKS)}, device_id_type=MESH)
    for k in range(1, SUBS):
        pl.semaphore_signal(barrier, inc=1, device_id={"sub": lax.rem(sub + k, SUBS)}, device_id_type=MESH)
    pl.semaphore_wait(barrier, RANKS + SUBS - 2)

    def pulse_copy(slot_src, slot_dst, peer, dst_sem):
        return pltpu.make_async_remote_copy(
            src_ref=pulses_ref.at[slot_src], dst_ref=held.at[slot_dst], send_sem=pulse_send.at[slot_src],
            recv_sem=pulse_recv.at[dst_sem], device_id={"rng": peer}, device_id_type=MESH,
        )

    for k in range(1, RANKS):
        peer = lax.rem(rng + k, RANKS)
        pulse_copy(peer, rng, peer, rng).start()
    own_pulses = pltpu.make_async_copy(pulses_ref.at[rng], held.at[rng], local_sem.at[0])
    own_pulses.start()

    for h in range(2):
        params[sub, 8 * h : 8 * h + 1, :] = off_ref[h : h + 1, :].astype(F32)
        params[sub, 8 * h + 1 : 8 * h + 5, :] = weight_ref[TAPS * h : TAPS * (h + 1), :]
        params[sub, 8 * h + 5 : 8 * h + 6, :] = rate_ref[h : h + 1, :]
        params[sub, 8 * h + 6 : 8 * h + 8, :] = jnp.zeros((2, ANGLES), F32)

    def param_copy(slot, peer):
        return pltpu.make_async_remote_copy(
            src_ref=params.at[slot], dst_ref=params.at[slot], send_sem=param_send.at[peer],
            recv_sem=param_recv.at[slot], device_id={"sub": peer}, device_id_type=MESH,
        )

    for k in range(1, SUBS):
        param_copy(sub, lax.rem(sub + k, SUBS)).start()

    real = steer_ref[0].astype(F32)
    imag = steer_ref[1].astype(F32)
    steer[:PSUB, :ANGLES] = real.T.astype(BF16)
    steer[:PSUB, ANGLES:] = imag.T.astype(BF16)
    steer[PSUB:, :ANGLES] = (-imag).T.astype(BF16)
    steer[PSUB:, ANGLES:] = real.T.astype(BF16)

    for k in range(1, SUBS):
        peer = lax.rem(sub + k, SUBS)
        param_copy(peer, peer).wait_recv()

    angle = lax.broadcasted_iota(jnp.int32, (1, ANGLES), 1).astype(F32)
    across = lax.broadcasted_iota(jnp.int32, (RADIX_B, ANGLES), 0).astype(F32)
    lane8 = lax.broadcasted_iota(jnp.int32, (8, ANGLES), 0)
    base = rng * BLOCK + sub * CHUNK

    def prepare(group, carry):
        for h in range(2):
            offset = params[group, 8 * h : 8 * h + 1, :]
            sources = [jnp.clip(angle + offset + float(t - 1), 0.0, ANGLES - 1.0) for t in range(TAPS)]
            weights = [params[group, 8 * h + 1 + t : 8 * h + 2 + t, :] for t in range(TAPS)]
            for part in range(ANGLES // RADIX_B):
                here = across + float(part * RADIX_B)
                total = jnp.zeros((RADIX_B, ANGLES), F32)
                for t in range(TAPS):
                    total = total + jnp.where(here == sources[t], weights[t], 0.0)
                band[2 * group + h, part * RADIX_B : (part + 1) * RADIX_B, :] = total.astype(BF16)
            rate = params[group, 8 * h + 5 : 8 * h + 6, :]
            at = rate * ((base + lane8).astype(F32) / SAMPLES)
            pr, pi = jnp.cos(at), jnp.sin(at)
            by = jnp.broadcast_to(rate * (8.0 / SAMPLES), (8, ANGLES))
            sr, si = jnp.cos(by), jnp.sin(by)
            for t in range(CHUNK // 8):
                rows = slice(8 * t, 8 * t + 8)
                qr, qi = pr, pi
                for level in range(LEVELS):
                    phase[level, 2 * group + h, 0, rows, :] = qr
                    phase[level, 2 * group + h, 1, rows, :] = qi
                    if level < LEVELS - 1:
                        qr, qi = times(qr, qi, pr, pi)
                pr, pi = times(pr, pi, sr, si)
        return carry

    lax.fori_loop(0, SUBS, prepare, 0)

    own_pulses.wait()
    for k in range(1, RANKS):
        peer = lax.rem(rng + k, RANKS)
        pulse_copy(peer, peer, peer, peer).wait_recv()

    for row in range(ROWS):
        for c in range(2):
            block = held[:, c, row].reshape(PSUB, RADIX_B)
            left[row * RADIX_B : (row + 1) * RADIX_B, c * PSUB : (c + 1) * PSUB] = block.T

    def image_copy(slot_src, slot_dst, peer):
        return pltpu.make_async_remote_copy(
            src_ref=sent.at[slot_src], dst_ref=image.at[0, slot_dst], send_sem=image_send.at[slot_src],
            recv_sem=image_recv.at[slot_dst], device_id={"sub": peer}, device_id_type=MESH,
        )

    for k in range(1, SUBS + 1):
        peer = lax.rem(sub + k, SUBS)
        bins = pl.ds(pl.multiple_of(peer * CHUNK, CHUNK), CHUNK)
        part = dot(left[bins, :], steer[...]).astype(BF16)
        for c in range(2):
            values = part[:, c * ANGLES : (c + 1) * ANGLES]
            if k < SUBS:
                sent[peer, c] = values
            else:
                image[0, sub, c] = values
        if k < SUBS:
            image_copy(peer, sub, peer).start()
    for k in range(1, SUBS):
        peer = lax.rem(sub + k, SUBS)
        image_copy(peer, peer, peer).wait_recv()

    def merge(level, group):
        now = level % 2
        far_group = partner_of(group, level)
        own = dot(image[now, group].reshape(2 * CHUNK, ANGLES), band[2 * group])
        far = dot(image[now, far_group].reshape(2 * CHUNK, ANGLES), band[2 * group + 1])
        ar, ai = times(own[:CHUNK], own[CHUNK:], phase[level, 2 * group, 0], phase[level, 2 * group, 1])
        br, bi = times(far[:CHUNK], far[CHUNK:], phase[level, 2 * group + 1, 0], phase[level, 2 * group + 1, 1])
        return ((ar + br).astype(BF16), (ai + bi).astype(BF16))

    for level in range(LEVELS - 1):

        def step(group, carry):
            real, imag = merge(level, group)
            image[(level + 1) % 2, group, 0] = real
            image[(level + 1) % 2, group, 1] = imag
            return carry

        lax.fori_loop(0, SUBS, step, 0)

    def tile_copy(slot_src, slot_dst, peer):
        return pltpu.make_async_remote_copy(
            src_ref=done.at[slot_src], dst_ref=out_ref.at[slot_dst], send_sem=tile_send.at[slot_src],
            recv_sem=tile_recv.at[slot_dst], device_id={"sub": peer}, device_id_type=MESH,
        )

    for k in range(1, SUBS + 1):
        peer = lax.rem(sub + k, SUBS)
        real, imag = merge(LEVELS - 1, peer)
        done[peer, 0] = real
        done[peer, 1] = imag
        if k < SUBS:
            tile_copy(peer, sub, peer).start()
    own_tile = pltpu.make_async_copy(done.at[sub], out_ref.at[sub], local_sem.at[1])
    own_tile.start()
    own_tile.wait()
    for k in range(1, SUBS):
        peer = lax.rem(sub + k, SUBS)
        tile_copy(peer, peer, peer).wait_recv()
    for k in range(1, RANKS):
        peer = lax.rem(rng + k, RANKS)
        pulse_copy(peer, rng, peer, rng).wait_send()
    for k in range(1, SUBS):
        peer = lax.rem(sub + k, SUBS)
        param_copy(sub, peer).wait_send()
        image_copy(peer, sub, peer).wait_send()
        tile_copy(peer, sub, peer).wait_send()


def tile_kernel(x_ref, out_ref):
    for c in range(2):
        image = x_ref[:, c].reshape(BLOCK, ANGLES)
        for row in range(ROWS):
            for part in range(ANGLES // RADIX_B):
                bins = slice(row * RADIX_B, (row + 1) * RADIX_B)
                angles = slice(part * RADIX_B, (part + 1) * RADIX_B)
                out_ref[angles, c, bins] = image[bins, angles].astype(F32).T


def vmem():
    return pl.BlockSpec(memory_space=pltpu.VMEM)


def local(echoes, filter_spectrum, range_shifts, steering, tap_offsets, tap_weights, phase_rates):
    rows = echoes.reshape(PULSES, 2, RADIX_A, RADIX_B).transpose(0, 2, 1, 3).reshape(-1, RADIX_B)
    filt = filter_spectrum.reshape(2, RADIX_A, RADIX_B).transpose(1, 0, 2).reshape(-1, RADIX_B)
    consts = [jnp.asarray(t) for t in tables()]
    pulses = pl.pallas_call(
        compress_kernel,
        out_shape=jax.ShapeDtypeStruct((RANKS, 2, ROWS, PULSES, RADIX_B), BF16),
        in_specs=[pl.BlockSpec(memory_space=pltpu.SMEM)] + [vmem()] * 7,
        out_specs=vmem(),
        scratch_shapes=[
            pltpu.VMEM((2, RADIX_A, RADIX_B), F32),
            pltpu.VMEM((2 * RADIX_A * PULSES, RADIX_B), F32),
        ],
        compiler_params=pltpu.CompilerParams(vmem_limit_bytes=32 << 20),
        name="compress",
    )(range_shifts, rows, filt, *consts)
    anywhere = pl.BlockSpec(memory_space=pl.ANY)
    dma = pltpu.SemaphoreType.DMA
    merged = pl.pallas_call(
        merge_kernel,
        out_shape=jax.ShapeDtypeStruct((SUBS, 2, CHUNK, ANGLES), BF16),
        in_specs=[anywhere] + [vmem()] * 4,
        out_specs=anywhere,
        scratch_shapes=[
            pltpu.VMEM((RANKS, 2, ROWS, PULSES, RADIX_B), BF16),
            pltpu.VMEM((SUBS, PARAMS, ANGLES), F32),
            pltpu.VMEM((BLOCK, 2 * PSUB), BF16),
            pltpu.VMEM((2 * PSUB, 2 * ANGLES), BF16),
            pltpu.VMEM((2 * SUBS, ANGLES, ANGLES), BF16),
            pltpu.VMEM((LEVELS, 2 * SUBS, 2, CHUNK, ANGLES), F32),
            pltpu.VMEM((SUBS, 2, CHUNK, ANGLES), BF16),
            pltpu.VMEM((2, SUBS, 2, CHUNK, ANGLES), BF16),
            pltpu.VMEM((SUBS, 2, CHUNK, ANGLES), BF16),
            dma((RANKS,)), dma((RANKS,)), dma((SUBS,)), dma((SUBS,)), dma((SUBS,)), dma((SUBS,)),
            dma((SUBS,)), dma((SUBS,)), dma((2,)),
        ],
        compiler_params=pltpu.CompilerParams(
            collective_id=0, has_side_effects=True, vmem_limit_bytes=56 << 20
        ),
        name="merge",
    )(
        pulses,
        steering.reshape(2, ANGLES, PSUB),
        tap_offsets.reshape(2, ANGLES),
        tap_weights.reshape(2 * TAPS, ANGLES),
        phase_rates.reshape(2, ANGLES),
    )
    return pl.pallas_call(
        tile_kernel,
        out_shape=jax.ShapeDtypeStruct((ANGLES, 2, BLOCK), F32),
        in_specs=[vmem()],
        out_specs=vmem(),
        compiler_params=pltpu.CompilerParams(vmem_limit_bytes=32 << 20),
        name="tile",
    )(merged)


def solution(mesh):
    placed = (
        P(("sub", "rng"), None, None),
        P(),
        P("sub"),
        P("sub", None, None, None),
        P("sub", None, None),
        P("sub", None, None, None),
        P("sub", None, None),
    )
    return jax.shard_map(
        local, mesh=mesh, in_specs=placed, out_specs=P("sub", None, "rng"), check_vma=False
    )
```

profile of v0, /device:TPU:8, one launch (start us, length us, event | category | flops | bytes accessed | tf_op | source)
XLA Modules:
  0.0 93.7 jit_solution(2630648201590566977)
XLA Ops:
  0.0 1.3 %reshape.30.weight_ref = f32[8,384]{1,0:T(8,128)} reshape(f32[1,2,4,384]{3,2,1,0:T(4,128)} %param.17) | data formatting | bytes 24576 | tf_op jit(solution)/shard_map/reshape | solution.py:385
  1.3 0.0 copy-start.2
  1.3 1.4 %copy-done.2 = f32[16,2,12288]{2,1,0:T(2,128)S(1)} copy-done((f32[16,2,12288]{2,1,0:T(2,128)S(1)}, f32[16,2,12288]{2,1,0:T(2,128)}, u32[]{:S(2)}) %copy-start.2) | copy-done | bytes 1572888
  2.7 0.0 copy-start.3
  2.7 0.9 %copy-done.3 = bf16[2,256,256]{2,1,0:T(8,128)(2,1)S(1)} copy-done((bf16[2,256,256]{2,1,0:T(8,128)(2,1)S(1)}, bf16[2,256,256]{2,1,0:T(8,128)(2,1)}, u32[]{:S(2)}) %copy-start.3) | copy-done | bytes 262168
  3.7 0.0 copy-start.4
  3.7 0.9 %copy-done.4 = bf16[2,256,256]{2,1,0:T(8,128)(2,1)S(1)} copy-done((bf16[2,256,256]{2,1,0:T(8,128)(2,1)S(1)}, bf16[2,256,256]{2,1,0:T(8,128)(2,1)}, u32[]{:S(2)}) %copy-start.4) | copy-done | bytes 262168
  4.6 0.0 copy-start.5
  4.6 0.9 copy-done.5
  5.5 0.0 copy-start.6
  5.5 0.9 copy-done.6
  6.5 0.0 copy-start.7
  6.5 0.9 copy-done.7
  7.4 0.0 copy-start.8
  7.4 0.9 copy-done.8
  8.3 0.0 copy-start.9
  8.3 0.7 copy-done.9
  9.0 11.0 %compress.1.pulses_ref = bf16[16,2,6,16,128]{4,3,2,1,0:T(8,128)(2,1)S(1)} custom-call(s32[256]{0:T(256)S(1)} %copy-done.9, f32[3072,128]{1,0:T(8,128)S(1)} %bitcast.13, f32[192,128]{1,0:T(8,128)S(1)} %bitcast.14, bf16[2,192,192]{2,1,0:T(8,128)(2,1)S(1)} %copy-done.7, bf16[2,256,256]{2,1,0:T(8,128)(2,1)S(1)} %copy-done.4, bf16[2,256,256]{2,1,0:T(8,128)(2,1)S(1)} %copy-done.3, ...), custom_call_target="tpu_custom_call" | custom-call | tf_op jit(solution)/shard_map/compress/pallas_call | solution.py:345
  20.0 0.0 copy-start.1
  20.0 0.9 copy-done.1
  20.9 68.8 %merge.1.x_ref = bf16[8,2,96,384]{3,2,1,0:T(8,128)(2,1)} custom-call(bf16[16,2,6,16,128]{4,3,2,1,0:T(8,128)(2,1)} %copy-done.1, bf16[2,384,256]{2,1,0:T(8,128)(2,1)} %bitcast.15, s32[2,384]{1,0:T(2,128)} %bitcast.16, f32[8,384]{1,0:T(8,128)} %reshape.30.weight_ref, f32[2,384]{1,0:T(2,128)} %bitcast.17), custom_call_target="tpu_custom_call" | custom-call | tf_op jit(solution)/shard_map/merge/pallas_call | solution.py:359
  89.7 0.0 copy-start
  89.7 1.3 %copy-done = bf16[8,2,96,384]{3,2,1,0:T(8,128)(2,1)S(1)} copy-done((bf16[8,2,96,384]{3,2,1,0:T(8,128)(2,1)S(1)}, bf16[8,2,96,384]{3,2,1,0:T(8,128)(2,1)}, u32[]{:S(2)}) %copy-start) | copy-done | bytes 1179672
  91.0 2.8 %tile.1 = f32[384,2,768]{2,1,0:T(2,128)} custom-call(bf16[8,2,96,384]{3,2,1,0:T(8,128)(2,1)S(1)} %copy-done), custom_call_target="tpu_custom_call" | custom-call | tf_op jit(solution)/shard_map/tile/pallas_call | solution.py:388
Async XLA Ops:
  1.3 1.4 %copy-start.2 = (f32[16,2,12288]{2,1,0:T(2,128)S(1)}, f32[16,2,12288]{2,1,0:T(2,128)}, u32[]{:S(2)}) copy-start(f32[16,2,12288]{2,1,0:T(2,128)} %param.12) | copy-start | bytes 4718596
  2.7 0.9 %copy-start.3 = (bf16[2,256,256]{2,1,0:T(8,128)(2,1)S(1)}, bf16[2,256,256]{2,1,0:T(8,128)(2,1)}, u32[]{:S(2)}) copy-start(bf16[2,256,256]{2,1,0:T(8,128)(2,1)} %constant.12.clone.vb) | copy-start | bytes 786436
  3.7 0.9 %copy-start.4 = (bf16[2,256,256]{2,1,0:T(8,128)(2,1)S(1)}, bf16[2,256,256]{2,1,0:T(8,128)(2,1)}, u32[]{:S(2)}) copy-start(bf16[2,256,256]{2,1,0:T(8,128)(2,1)} %constant.11.clone.wb) | copy-start | bytes 786436
  4.6 0.9 copy-start.5
  5.5 0.9 copy-start.6
  6.5 0.9 copy-start.7
  7.4 0.9 copy-start.8
  8.3 0.7 copy-start.9
  20.0 0.9 copy-start.1
  89.7 1.3 %copy-start = (bf16[8,2,96,384]{3,2,1,0:T(8,128)(2,1)S(1)}, bf16[8,2,96,384]{3,2,1,0:T(8,128)(2,1)}, u32[]{:S(2)}) copy-start(bf16[8,2,96,384]{3,2,1,0:T(8,128)(2,1)} %merge.1.x_ref) | copy-start | bytes 3538948
where the time goes:
time: 94.2 us; the launch traced here: 93.7 us
  Pallas kernels  82.6 us (88%)
  local copies, waits for them, and re-layouts  11.1 us (12%)
    pallas_call x1, Pallas kernels, local(): pl.pallas_call(merge_kernel, out_shape=jax.ShapeDtypeStruct((SUBS, 2, CHU...  68.8 us
    pallas_call x1, Pallas kernels, local(): pl.pallas_call(compress_kernel, out_shape=jax.ShapeDtypeStruct((RANKS, 2,...  11 us
    unnamed x20, local copies, waits for them, and re-layouts  9.79 us
    pallas_call x1, Pallas kernels, local(): pl.pallas_call(tile_kernel, out_shape=jax.ShapeDtypeStruct((ANGLES, 2, BL...  2.77 us

commit v1 on v0

v1 whole, which is shorter than its diff:
```python
import math

import jax
import jax.numpy as jnp
import ml_dtypes
import numpy as np
from jax import lax
from jax.experimental import pallas as pl
from jax.experimental.pallas import tpu as pltpu
from jax.sharding import PartitionSpec as P

RADIX_A = 96
RADIX_B = 128
ANGLES = 384
TAPS = 4
SAMPLES = 12288
SUBS = 8
RANKS = 16
PULSES = 16
PSUB = RANKS * PULSES
BLOCK = SAMPLES // RANKS
ROWS = BLOCK // RADIX_B
STAGES = 2
STAGE_ROWS = ROWS // STAGES
STAGE_BINS = BLOCK // STAGES
PIECE = STAGE_BINS // SUBS
PAIRS = 2
STEPS = PULSES // (2 * PAIRS)
HALO = 16
LEVELS = 3
PARAMS = 16
MESH = pl.DeviceIdType.MESH
F32 = jnp.float32
BF16 = jnp.bfloat16


def halves(table, axis):
    high = table.astype(np.float32).astype(ml_dtypes.bfloat16)
    low = (table - high.astype(np.float64)).astype(np.float32).astype(ml_dtypes.bfloat16)
    return np.concatenate([high, high, low], axis=axis)


def tables():
    a = np.arange(RADIX_A)
    b = np.arange(RADIX_B)
    wa = np.exp(-2j * np.pi / RADIX_A * (np.outer(a, a) % RADIX_A))
    wb = np.exp(-2j * np.pi / RADIX_B * (np.outer(b, b) % RADIX_B))
    order = 4 * (b % 32) + b // 32
    wb = wb[:, order]
    vb = np.conj(wb.T)
    va = np.conj(wa)
    left = lambda w: halves(np.block([[w.real, -w.imag], [w.imag, w.real]]), 1)
    right = lambda w: halves(np.block([[w.real, w.imag], [-w.imag, w.real]]), 0)
    turn = np.exp(-2j * np.pi / SAMPLES * np.outer(a, b))
    shifts = np.arange(-HALO, HALO + 1)
    back = np.exp(2j * np.pi / SAMPLES * a[None, :, None] * (b[None, None, :] + shifts[:, None, None])) / SAMPLES
    columns = np.exp(2j * np.pi / RADIX_B * (np.outer(shifts, order) % RADIX_B))
    lanes = np.zeros((2 * HALO + 1, 8, RADIX_B))
    lanes[:, 0], lanes[:, 1] = columns.real, columns.imag
    return (
        left(wa),
        right(wb),
        right(vb),
        left(va),
        np.stack([turn.real, turn.imag]).astype(np.float32),
        np.stack([back.real, back.imag], axis=1).astype(np.float32),
        lanes.astype(np.float32),
    )


def split(x):
    high = x.astype(BF16)
    return high, (x - high.astype(F32)).astype(BF16)


def dot(left, right):
    return jnp.dot(left, right, preferred_element_type=F32)


def left_product(table, x):
    high, low = split(x)
    return dot(table, jnp.concatenate([high, low, high], axis=0))


def right_product(x, table):
    high, low = split(x)
    return dot(jnp.concatenate([high, low, high], axis=1), table)


def times(ar, ai, br, bi):
    return ar * br - ai * bi, ar * bi + ai * br


def load_filter(f_ref, filt):
    lane32 = lax.broadcasted_iota(jnp.int32, (32, RADIX_B), 1)
    for c in range(2):
        f0, f1, f2 = (f_ref[pl.ds(2 * e + c, 32, stride=6), :] for e in range(3))
        parts = [
            f0,
            jnp.where(lane32 < 32, pltpu.roll(f0, 32, 1), pltpu.roll(f1, 32, 1)),
            jnp.where(lane32 < 64, pltpu.roll(f1, 64, 1), pltpu.roll(f2, 64, 1)),
            pltpu.roll(f2, 96, 1),
        ]
        filt[c] = jnp.concatenate(parts, axis=0).T[:RADIX_A]


def compress(i, first, shift_ref, x_ref, filt, wa, wb, vb, va, tw, back, lanes, rows):
    pairs = range(PAIRS)
    pulse = [[(i * PAIRS + j) * 2 + q for q in range(2)] for j in pairs]
    shift = [[shift_ref[first + p] for p in two] for two in pulse]
    results = []
    for j in pairs:
        signal = []
        for q in range(2):
            start = pulse[j][q] * 2 * RADIX_A
            halves = [x_ref[pl.ds(start + c, RADIX_A, stride=2), :] for c in range(2)]
            signal.append(jnp.concatenate(halves, axis=0))
        results.append(left_product(wa[...], jnp.concatenate(signal, axis=1)))
    for j in pairs:
        turned = []
        for q in range(2):
            part = results[j][:, q * RADIX_B : (q + 1) * RADIX_B]
            turned.append(jnp.concatenate(times(part[:RADIX_A], part[RADIX_A:], tw[0], tw[1]), axis=1))
        results[j] = right_product(jnp.concatenate(turned, axis=0), wb[...])
    for j in pairs:
        turned = []
        for q in range(2):
            part = results[j][q * RADIX_A : (q + 1) * RADIX_A]
            at = shift[j][q] + HALO
            gain = times(filt[0], filt[1], lanes[at, 0:1, :], lanes[at, 1:2, :])
            turned.append(jnp.concatenate(times(part[:, :RADIX_B], part[:, RADIX_B:], *gain), axis=1))
        results[j] = right_product(jnp.concatenate(turned, axis=0), vb[...])
    for j in pairs:
        turned = []
        for q in range(2):
            part = results[j][q * RADIX_A : (q + 1) * RADIX_A]
            at = shift[j][q] + HALO
            values = times(part[:, :RADIX_B], part[:, RADIX_B:], back[at, 0], back[at, 1])
            turned.append(jnp.concatenate(values, axis=0))
        results[j] = left_product(va[...], jnp.concatenate(turned, axis=1))
    bin8 = lax.broadcasted_iota(jnp.int32, (8, RADIX_B), 0) * RADIX_B
    bin8 = bin8 + lax.broadcasted_iota(jnp.int32, (8, RADIX_B), 1)
    for j in pairs:
        for q in range(2):
            s = shift[j][q]
            for c in range(2):
                values = results[j][c * RADIX_A : (c + 1) * RADIX_A, q * RADIX_B : (q + 1) * RADIX_B]
                top = jnp.where(bin8 + s >= 0, values[:8], 0.0)
                end = jnp.where(bin8 + s < 8 * RADIX_B, values[RADIX_A - 8 :], 0.0)
                values = jnp.concatenate([top, values[8 : RADIX_A - 8], end], axis=0)
                start = c * RADIX_A * PULSES + pulse[j][q]
                rows[pl.ds(start, RADIX_A, stride=PULSES), :] = values


def kernel(
    shift_hbm, x_hbm, f_hbm, steer_hbm, off_hbm, weight_hbm, rate_hbm,
    wa_hbm, wb_hbm, vb_hbm, va_hbm, tw_hbm, back_hbm, lanes_hbm, out_ref,
    shift_ref, x_ref, f_ref, steer_ref, off_ref, weight_ref, rate_ref, wa, wb, vb, va, tw, back, lanes,
    filt, rows, pulses, held, params, left, steer, band, phase, sent, image,
    load_sem, echo_sem, pulse_send, pulse_recv, param_send, param_recv, image_send, image_recv, tile_send, tile_recv,
    local_sem,
):
    sub = lax.axis_index("sub")
    rng = lax.axis_index("rng")
    barrier = pltpu.get_barrier_semaphore()
    for k in range(1, RANKS):
        pl.semaphore_signal(barrier, inc=1, device_id={"rng": lax.rem(rng + k, RANKS)}, device_id_type=MESH)
    for k in range(1, SUBS):
        pl.semaphore_signal(barrier, inc=1, device_id={"sub": lax.rem(sub + k, SUBS)}, device_id_type=MESH)

    step_rows = PAIRS * 4 * RADIX_A

    def echo_copy(i):
        part = pl.ds(pl.multiple_of(i * step_rows, step_rows), step_rows)
        return pltpu.make_async_copy(x_hbm.at[part], x_ref.at[part], echo_sem.at[i])

    def load(n, src, dst):
        return pltpu.make_async_copy(src, dst, load_sem.at[n])

    first_loads = [
        load(n, src, dst)
        for n, (src, dst) in enumerate(
            [(wa_hbm, wa), (tw_hbm, tw), (f_hbm, f_ref), (shift_hbm, shift_ref), (wb_hbm, wb), (vb_hbm, vb),
             (lanes_hbm, lanes), (va_hbm, va), (back_hbm, back)]
        )
    ]
    late_loads = [
        load(len(first_loads) + n, src, dst)
        for n, (src, dst) in enumerate(
            [(steer_hbm, steer_ref), (off_hbm, off_ref), (weight_hbm, weight_ref), (rate_hbm, rate_ref)]
        )
    ]
    echo_copy(0).start()
    for copy in first_loads:
        copy.start()
    for i in range(1, STEPS):
        echo_copy(i).start()
    for copy in late_loads:
        copy.start()
    for copy in first_loads:
        copy.wait()
    load_filter(f_ref, filt)

    def filter_step(i, carry):
        echo_copy(i).wait()
        compress(i, rng * PULSES, shift_ref, x_ref, filt, wa, wb, vb, va, tw, back, lanes, rows)
        return carry

    lax.fori_loop(0, STEPS, filter_step, 0)

    def pack(j, carry):
        for stage in range(STAGES):
            for c in range(2):
                start = (c * RADIX_A + j * ROWS + stage * STAGE_ROWS) * PULSES
                block = rows[pl.ds(pl.multiple_of(start, PULSES), STAGE_ROWS * PULSES), :].astype(BF16)
                pulses[stage, j, c] = block.reshape(STAGE_ROWS, PULSES, RADIX_B)
        return carry

    lax.fori_loop(0, RANKS, pack, 0)

    pl.semaphore_wait(barrier, RANKS + SUBS - 2)

    def pulse_copy(stage, src, dst, peer):
        return pltpu.make_async_remote_copy(
            src_ref=pulses.at[stage, src], dst_ref=held.at[stage, dst], send_sem=pulse_send.at[stage, src],
            recv_sem=pulse_recv.at[stage, dst], device_id={"rng": peer}, device_id_type=MESH,
        )

    def own_pulses(stage):
        return pltpu.make_async_copy(pulses.at[stage, rng], held.at[stage, rng], local_sem.at[stage])

    for stage in range(STAGES):

        def send_pulses(k, carry):
            peer = lax.rem(rng + k, RANKS)
            pulse_copy(stage, peer, rng, peer).start()
            return carry

        lax.fori_loop(1, RANKS, send_pulses, 0)
        own_pulses(stage).start()

    for copy in late_loads:
        copy.wait()
    for h in range(2):
        params[sub, 8 * h : 8 * h + 1, :] = off_ref[h : h + 1, :].astype(F32)
        params[sub, 8 * h + 1 : 8 * h + 5, :] = weight_ref[h]
        params[sub, 8 * h + 5 : 8 * h + 6, :] = rate_ref[h : h + 1, :]
        params[sub, 8 * h + 6 : 8 * h + 8, :] = jnp.zeros((2, ANGLES), F32)

    def param_copy(slot, peer):
        return pltpu.make_async_remote_copy(
            src_ref=params.at[slot], dst_ref=params.at[slot], send_sem=param_send.at[peer],
            recv_sem=param_recv.at[slot], device_id={"sub": peer}, device_id_type=MESH,
        )

    for k in range(1, SUBS):
        param_copy(sub, lax.rem(sub + k, SUBS)).start()

    real = steer_ref[0].astype(F32)
    imag = steer_ref[1].astype(F32)
    steer[:PSUB, :ANGLES] = real.T.astype(BF16)
    steer[:PSUB, ANGLES:] = imag.T.astype(BF16)
    steer[PSUB:, :ANGLES] = (-imag).T.astype(BF16)
    steer[PSUB:, ANGLES:] = real.T.astype(BF16)

    for k in range(1, SUBS):
        peer = lax.rem(sub + k, SUBS)
        param_copy(peer, peer).wait_recv()

    angle = lax.broadcasted_iota(jnp.int32, (1, ANGLES), 1).astype(F32)
    across = lax.broadcasted_iota(jnp.int32, (RADIX_B, ANGLES), 0).astype(F32)
    row8 = lax.broadcasted_iota(jnp.int32, (8, ANGLES), 0)
    base = rng * BLOCK + sub * PIECE

    def prepare(group, carry):
        for h in range(2):
            offset = params[group, 8 * h : 8 * h + 1, :]
            sources = [jnp.clip(angle + offset + float(t - 1), 0.0, ANGLES - 1.0) for t in range(TAPS)]
            weights = [params[group, 8 * h + 1 + t : 8 * h + 2 + t, :] for t in range(TAPS)]
            for part in range(ANGLES // RADIX_B):
                here = across + float(part * RADIX_B)
                total = jnp.zeros((RADIX_B, ANGLES), F32)
                for t in range(TAPS):
                    total = total + jnp.where(here == sources[t], weights[t], 0.0)
                band[2 * group + h, part * RADIX_B : (part + 1) * RADIX_B, :] = total.astype(BF16)
            rate = params[group, 8 * h + 5 : 8 * h + 6, :]
            by = jnp.broadcast_to(rate * (8.0 / SAMPLES), (8, ANGLES))
            sr, si = jnp.cos(by), jnp.sin(by)
            for stage in range(STAGES):
                at = rate * ((base + stage * STAGE_BINS + row8).astype(F32) / SAMPLES)
                pr, pi = jnp.cos(at), jnp.sin(at)
                for t in range(PIECE // 8):
                    part = slice(8 * t, 8 * t + 8)
                    qr, qi = pr, pi
                    for level in range(LEVELS):
                        phase[stage * LEVELS + level, 2 * group + h, 0, part, :] = qr
                        phase[stage * LEVELS + level, 2 * group + h, 1, part, :] = qi
                        if level < LEVELS - 1:
                            qr, qi = times(qr, qi, pr, pi)
                    if t < PIECE // 8 - 1:
                        pr, pi = times(pr, pi, sr, si)
        return carry

    lax.fori_loop(0, SUBS, prepare, 0)

    def image_copy(stage, src, dst, peer):
        return pltpu.make_async_remote_copy(
            src_ref=sent.at[stage, src], dst_ref=image.at[stage, 0, dst], send_sem=image_send.at[stage, src],
            recv_sem=image_recv.at[stage, dst], device_id={"sub": peer}, device_id_type=MESH,
        )

    def own_image(stage):
        return pltpu.make_async_copy(sent.at[stage, sub], image.at[stage, 0, sub], local_sem.at[STAGES + stage])

    for stage in range(STAGES):

        def pulses_here(k, carry):
            peer = lax.rem(rng + k, RANKS)
            pulse_copy(stage, peer, peer, peer).wait_recv()
            return carry

        lax.fori_loop(1, RANKS, pulses_here, 0)
        own_pulses(stage).wait()
        for row in range(STAGE_ROWS):
            for c in range(2):
                block = held[stage, :, c, row].reshape(PSUB, RADIX_B)
                left[stage, row * RADIX_B : (row + 1) * RADIX_B, c * PSUB : (c + 1) * PSUB] = block.T

        def make_image(k, carry):
            peer = lax.rem(sub + k, SUBS)
            bins = pl.ds(pl.multiple_of(peer * PIECE, PIECE), PIECE)
            part = dot(left[stage, bins, :], steer[...]).astype(BF16)
            for c in range(2):
                sent[stage, peer, c] = part[:, c * ANGLES : (c + 1) * ANGLES]

            @pl.when(k < SUBS)
            def _():
                image_copy(stage, peer, sub, peer).start()

            return carry

        lax.fori_loop(1, SUBS + 1, make_image, 0)
        own_image(stage).start()

    def tile_copy(stage, src, dst, peer):
        return pltpu.make_async_remote_copy(
            src_ref=image.at[stage, 1, src], dst_ref=out_ref.at[stage, dst], send_sem=tile_send.at[stage, src],
            recv_sem=tile_recv.at[stage, dst], device_id={"sub": peer}, device_id_type=MESH,
        )

    def own_tile(stage):
        return pltpu.make_async_copy(
            image.at[stage, 1, sub], out_ref.at[stage, sub], local_sem.at[2 * STAGES + stage]
        )

    for stage in range(STAGES):

        def image_here(k, carry):
            peer = lax.rem(sub + k, SUBS)
            image_copy(stage, peer, peer, peer).wait_recv()
            return carry

        lax.fori_loop(1, SUBS, image_here, 0)
        own_image(stage).wait()

        def merge(i, carry):
            level = i // SUBS
            k = lax.rem(i, SUBS) + 1
            group = lax.rem(sub + k, SUBS)
            now = lax.rem(level, 2)
            bit = 1 + level + level // 2
            far_group = group + bit - 2 * bit * lax.rem(group // bit, 2)
            turn = phase.at[stage * LEVELS + level]
            own = dot(image[stage, now, group].reshape(2 * PIECE, ANGLES), band[2 * group])
            far = dot(image[stage, now, far_group].reshape(2 * PIECE, ANGLES), band[2 * group + 1])
            ar, ai = times(own[:PIECE], own[PIECE:], turn[2 * group, 0], turn[2 * group, 1])
            br, bi = times(far[:PIECE], far[PIECE:], turn[2 * group + 1, 0], turn[2 * group + 1, 1])
            image[stage, 1 - now, group, 0] = (ar + br).astype(BF16)
            image[stage, 1 - now, group, 1] = (ai + bi).astype(BF16)

            @pl.when(jnp.logical_and(level == LEVELS - 1, k < SUBS))
            def _():
                tile_copy(stage, group, sub, group).start()

            return carry

        lax.fori_loop(0, LEVELS * SUBS, merge, 0)
        own_tile(stage).start()

    for stage in range(STAGES):

        def finish(k, carry):
            peer = lax.rem(sub + k, SUBS)
            tile_copy(stage, peer, peer, peer).wait_recv()
            tile_copy(stage, peer, sub, peer).wait_send()
            image_copy(stage, peer, sub, peer).wait_send()
            return carry

        lax.fori_loop(1, SUBS, finish, 0)
        own_tile(stage).wait()

        def pulses_gone(k, carry):
            peer = lax.rem(rng + k, RANKS)
            pulse_copy(stage, peer, rng, peer).wait_send()
            return carry

        lax.fori_loop(1, RANKS, pulses_gone, 0)
    for k in range(1, SUBS):
        param_copy(sub, lax.rem(sub + k, SUBS)).wait_send()


def tile_kernel(x_ref, out_ref):
    for stage in range(STAGES):
        for c in range(2):
            image = x_ref[stage, :, c].reshape(STAGE_BINS, ANGLES)
            for row in range(STAGE_ROWS):
                for part in range(ANGLES // RADIX_B):
                    angles = slice(part * RADIX_B, (part + 1) * RADIX_B)
                    start = stage * STAGE_BINS + row * RADIX_B
                    values = image[row * RADIX_B : (row + 1) * RADIX_B, angles]
                    out_ref[angles, c, start : start + RADIX_B] = values.astype(F32).T


def local(echoes, filter_spectrum, range_shifts, steering, tap_offsets, tap_weights, phase_rates):
    rows = echoes.reshape(PULSES, 2, RADIX_A, RADIX_B).transpose(0, 2, 1, 3).reshape(-1, RADIX_B)
    filt = filter_spectrum.reshape(2, RADIX_A, RADIX_B).transpose(1, 0, 2).reshape(-1, RADIX_B)
    consts = [jnp.asarray(t) for t in tables()]
    operands = [
        range_shifts,
        rows,
        filt,
        steering.reshape(2, ANGLES, PSUB),
        tap_offsets.reshape(2, ANGLES),
        tap_weights.reshape(2, TAPS, ANGLES),
        phase_rates.reshape(2, ANGLES),
        *consts,
    ]
    hbm = pl.BlockSpec(memory_space=pltpu.HBM)
    dma = pltpu.SemaphoreType.DMA
    landing = [pltpu.SMEM((PSUB,), jnp.int32)] + [pltpu.VMEM(x.shape, x.dtype) for x in operands[1:]]
    merged = pl.pallas_call(
        kernel,
        out_shape=jax.ShapeDtypeStruct((STAGES, SUBS, 2, PIECE, ANGLES), BF16),
        in_specs=[hbm] * len(operands),
        out_specs=hbm,
        scratch_shapes=[
            *landing,
            pltpu.VMEM((2, RADIX_A, RADIX_B), F32),
            pltpu.VMEM((2 * RADIX_A * PULSES, RADIX_B), F32),
            pltpu.VMEM((STAGES, RANKS, 2, STAGE_ROWS, PULSES, RADIX_B), BF16),
            pltpu.VMEM((STAGES, RANKS, 2, STAGE_ROWS, PULSES, RADIX_B), BF16),
            pltpu.VMEM((SUBS, PARAMS, ANGLES), F32),
            pltpu.VMEM((STAGES, STAGE_BINS, 2 * PSUB), BF16),
            pltpu.VMEM((2 * PSUB, 2 * ANGLES), BF16),
            pltpu.VMEM((2 * SUBS, ANGLES, ANGLES), BF16),
            pltpu.VMEM((STAGES * LEVELS, 2 * SUBS, 2, PIECE, ANGLES), F32),
            pltpu.VMEM((STAGES, SUBS, 2, PIECE, ANGLES), BF16),
            pltpu.VMEM((STAGES, 2, SUBS, 2, PIECE, ANGLES), BF16),
            dma((len(operands),)), dma((STEPS,)), dma((STAGES, RANKS)), dma((STAGES, RANKS)), dma((SUBS,)), dma((SUBS,)),
            dma((STAGES, SUBS)), dma((STAGES, SUBS)), dma((STAGES, SUBS)), dma((STAGES, SUBS)), dma((3 * STAGES,)),
        ],
        compiler_params=pltpu.CompilerParams(
            collective_id=0, has_side_effects=True, vmem_limit_bytes=56 << 20
        ),
        name="merge",
    )(*operands)
    vmem = pl.BlockSpec(memory_space=pltpu.VMEM)
    return pl.pallas_call(
        tile_kernel,
        out_shape=jax.ShapeDtypeStruct((ANGLES, 2, BLOCK), F32),
        in_specs=[vmem],
        out_specs=vmem,
        compiler_params=pltpu.CompilerParams(vmem_limit_bytes=32 << 20),
        name="tile",
    )(merged)


def solution(mesh):
    placed = (
        P(("sub", "rng"), None, None),
        P(),
        P("sub"),
        P("sub", None, None, None),
        P("sub", None, None),
        P("sub", None, None, None),
        P("sub", None, None),
    )
    return jax.shard_map(
        local, mesh=mesh, in_specs=placed, out_specs=P("sub", None, "rng"), check_vma=False
    )
```

time: 94.2 us -> 67 us (0.71)
  Pallas kernels: 82.6 us -> 64.7 us
  local copies, waits for them, and re-layouts: 11.1 us -> 1.26 us
    pallas_call x2 -> x1, Pallas kernels: 79.8 us -> 61.9 us  [local(): pl.pallas_call(kernel, out_shape=jax.ShapeDtypeStruct((STAGES, SUBS, 2, P...]
    unnamed x20 -> x2, local copies, waits for them, and re-layouts: 9.79 us -> 1.26 us
    reshape x1 -> x0, local copies, waits for them, and re-layouts: 1.31 us -> none  [local(): tap_weights.reshape(2 * TAPS, ANGLES)]
where the time goes in v1:
time: 67 us; the launch traced here: 65.9 us
  Pallas kernels  64.7 us (97%)
  local copies, waits for them, and re-layouts  1.26 us (2%)
    pallas_call x1, Pallas kernels, local(): pl.pallas_call(kernel, out_shape=jax.ShapeDtypeStruct((STAGES, SUBS, 2, P...  61.9 us
    pallas_call x1, Pallas kernels, local(): pl.pallas_call(tile_kernel, out_shape=jax.ShapeDtypeStruct((ANGLES, 2, BL...  2.77 us

profile of v1, /device:TPU:8, one launch (start us, length us, event | category | flops | bytes accessed | tf_op | source)
XLA Modules:
  0.0 65.9 jit_solution(16075886172426746109)
XLA Ops:
  0.0 61.9 %merge.1.x_ref = bf16[2,8,2,48,384]{4,3,2,1,0:T(8,128)(2,1)} custom-call(s32[256]{0:T(256)} %shift_hbm.1, f32[3072,128]{1,0:T(8,128)} %bitcast.14, f32[192,128]{1,0:T(8,128)} %bitcast.16, bf16[2,384,256]{2,1,0:T(8,128)(2,1)} %bitcast.15, s32[2,384]{1,0:T(2,128)} %bitcast.18, f32[2,4,384]{2,1,0:T(4,128)} %bitcast.17, f32[2,384]{1,0:T(2,128)} %bitcast.19, ...), custom_call_target="tpu_custom_call" | custom-call | tf_op jit(solution)/shard_map/merge/pallas_call | solution.py:441
  61.9 0.0 copy-start
  61.9 1.3 %copy-done = bf16[2,8,2,48,384]{4,3,2,1,0:T(8,128)(2,1)S(1)} copy-done((bf16[2,8,2,48,384]{4,3,2,1,0:T(8,128)(2,1)S(1)}, bf16[2,8,2,48,384]{4,3,2,1,0:T(8,128)(2,1)}, u32[]{:S(2)}) %copy-start) | copy-done | bytes 1179672
  63.2 2.8 %tile.1 = f32[384,2,768]{2,1,0:T(2,128)} custom-call(bf16[2,8,2,48,384]{4,3,2,1,0:T(8,128)(2,1)S(1)} %copy-done), custom_call_target="tpu_custom_call" | custom-call | tf_op jit(solution)/shard_map/tile/pallas_call | solution.py:468
Async XLA Ops:
  61.9 1.3 %copy-start = (bf16[2,8,2,48,384]{4,3,2,1,0:T(8,128)(2,1)S(1)}, bf16[2,8,2,48,384]{4,3,2,1,0:T(8,128)(2,1)}, u32[]{:S(2)}) copy-start(bf16[2,8,2,48,384]{4,3,2,1,0:T(8,128)(2,1)} %merge.1.x_ref) | copy-start | bytes 3538948

commit v2 on v1

--- a/solution.py
+++ b/solution.py
@@ -24,8 +24,8 @@
 STAGE_ROWS = ROWS // STAGES
 STAGE_BINS = BLOCK // STAGES
 PIECE = STAGE_BINS // SUBS
-PAIRS = 2
-STEPS = PULSES // (2 * PAIRS)
+TOGETHER = 8
+ECHO_PARTS = 4
 HALO = 16
 LEVELS = 3
 PARAMS = 16
@@ -104,24 +104,34 @@
         filt[c] = jnp.concatenate(parts, axis=0).T[:RADIX_A]
 
 
-def compress(i, first, shift_ref, x_ref, filt, wa, wb, vb, va, tw, back, lanes, rows):
-    pairs = range(PAIRS)
-    pulse = [[(i * PAIRS + j) * 2 + q for q in range(2)] for j in pairs]
-    shift = [[shift_ref[first + p] for p in two] for two in pulse]
+def compress(first, arrived, shift_ref, x_ref, f_ref, filt, wa, wb, vb, va, tw, back, lanes, rows):
+    pairs = range(PULSES // 2)
+    pulse = [[2 * j + q for q in range(2)] for j in pairs]
     results = []
+    arrived("wa")
+    arrived("tw")
     for j in pairs:
+        if j % 2 == 0:
+            arrived(j // 2)
         signal = []
         for q in range(2):
             start = pulse[j][q] * 2 * RADIX_A
             halves = [x_ref[pl.ds(start + c, RADIX_A, stride=2), :] for c in range(2)]
             signal.append(jnp.concatenate(halves, axis=0))
         results.append(left_product(wa[...], jnp.concatenate(signal, axis=1)))
+    arrived("wb")
     for j in pairs:
         turned = []
         for q in range(2):
             part = results[j][:, q * RADIX_B : (q + 1) * RADIX_B]
             turned.append(jnp.concatenate(times(part[:RADIX_A], part[RADIX_A:], tw[0], tw[1]), axis=1))
         results[j] = right_product(jnp.concatenate(turned, axis=0), wb[...])
+    arrived("filter")
+    arrived("shift")
+    arrived("lanes")
+    arrived("vb")
+    load_filter(f_ref, filt)
+    shift = [[shift_ref[first + p] for p in two] for two in pulse]
     for j in pairs:
         turned = []
         for q in range(2):
@@ -130,6 +140,8 @@
             gain = times(filt[0], filt[1], lanes[at, 0:1, :], lanes[at, 1:2, :])
             turned.append(jnp.concatenate(times(part[:, :RADIX_B], part[:, RADIX_B:], *gain), axis=1))
         results[j] = right_product(jnp.concatenate(turned, axis=0), vb[...])
+    arrived("back")
+    arrived("va")
     for j in pairs:
         turned = []
         for q in range(2):
@@ -156,7 +168,7 @@
     shift_hbm, x_hbm, f_hbm, steer_hbm, off_hbm, weight_hbm, rate_hbm,
     wa_hbm, wb_hbm, vb_hbm, va_hbm, tw_hbm, back_hbm, lanes_hbm, out_ref,
     shift_ref, x_ref, f_ref, steer_ref, off_ref, weight_ref, rate_ref, wa, wb, vb, va, tw, back, lanes,
-    filt, rows, pulses, held, params, left, steer, band, phase, sent, image,
+    filt, rows, pulses, held, params, rates, turns, left, steer, band, phase, sent, image,
     load_sem, echo_sem, pulse_send, pulse_recv, param_send, param_recv, image_send, image_recv, tile_send, tile_recv,
     local_sem,
 ):
@@ -168,45 +180,35 @@
     for k in range(1, SUBS):
         pl.semaphore_signal(barrier, inc=1, device_id={"sub": lax.rem(sub + k, SUBS)}, device_id_type=MESH)
 
-    step_rows = PAIRS * 4 * RADIX_A
+    echo_rows = x_ref.shape[0] // ECHO_PARTS
 
     def echo_copy(i):
-        part = pl.ds(pl.multiple_of(i * step_rows, step_rows), step_rows)
+        part = pl.ds(i * echo_rows, echo_rows)
         return pltpu.make_async_copy(x_hbm.at[part], x_ref.at[part], echo_sem.at[i])
 
     def load(n, src, dst):
         return pltpu.make_async_copy(src, dst, load_sem.at[n])
 
-    first_loads = [
-        load(n, src, dst)
-        for n, (src, dst) in enumerate(
-            [(wa_hbm, wa), (tw_hbm, tw), (f_hbm, f_ref), (shift_hbm, shift_ref), (wb_hbm, wb), (vb_hbm, vb),
-             (lanes_hbm, lanes), (va_hbm, va), (back_hbm, back)]
-        )
+    names = ["wa", "tw", "wb", "filter", "shift", "lanes", "vb", "va", "back"]
+    arrays = [
+        (wa_hbm, wa), (tw_hbm, tw), (wb_hbm, wb), (f_hbm, f_ref), (shift_hbm, shift_ref), (lanes_hbm, lanes),
+        (vb_hbm, vb), (va_hbm, va), (back_hbm, back), (steer_hbm, steer_ref), (off_hbm, off_ref),
+        (weight_hbm, weight_ref), (rate_hbm, rate_ref),
     ]
-    late_loads = [
-        load(len(first_loads) + n, src, dst)
-        for n, (src, dst) in enumerate(
-            [(steer_hbm, steer_ref), (off_hbm, off_ref), (weight_hbm, weight_ref), (rate_hbm, rate_ref)]
-        )
-    ]
-    echo_copy(0).start()
-    for copy in first_loads:
-        copy.start()
-    for i in range(1, STEPS):
-        echo_copy(i).start()
+    copies = [load(n, src, dst) for n, (src, dst) in enumerate(arrays)]
+    late_loads = copies[len(names) :]
+    loads = dict(zip(names, copies))
+    loads.update({i: echo_copy(i) for i in range(ECHO_PARTS)})
+    order = ["wa", 0, "tw", 1, "wb", 2, 3, "filter", "shift", "lanes", "vb", "va", "back"]
+    for name in order:
+        loads[name].start()
     for copy in late_loads:
         copy.start()
-    for copy in first_loads:
-        copy.wait()
-    load_filter(f_ref, filt)
-
-    def filter_step(i, carry):
-        echo_copy(i).wait()
-        compress(i, rng * PULSES, shift_ref, x_ref, filt, wa, wb, vb, va, tw, back, lanes, rows)
-        return carry
-
-    lax.fori_loop(0, STEPS, filter_step, 0)
+
+    def arrived(name):
+        loads[name].wait()
+
+    compress(rng * PULSES, arrived, shift_ref, x_ref, f_ref, filt, wa, wb, vb, va, tw, back, lanes, rows)
 
     def pack(j, carry):
         for stage in range(STAGES):
@@ -239,6 +241,12 @@
         lax.fori_loop(1, RANKS, send_pulses, 0)
         own_pulses(stage).start()
 
+    def clear(which, carry):
+        band[which] = jnp.zeros((2, 2 * RADIX_B, 2 * RADIX_B), BF16)
+        return carry
+
+    lax.fori_loop(0, 2 * SUBS, clear, 0)
+
     for copy in late_loads:
         copy.wait()
     for h in range(2):
@@ -268,40 +276,71 @@
         param_copy(peer, peer).wait_recv()
 
     angle = lax.broadcasted_iota(jnp.int32, (1, ANGLES), 1).astype(F32)
-    across = lax.broadcasted_iota(jnp.int32, (RADIX_B, ANGLES), 0).astype(F32)
+    across = lax.broadcasted_iota(jnp.int32, (RADIX_B, RADIX_B), 0).astype(F32)
     row8 = lax.broadcasted_iota(jnp.int32, (8, ANGLES), 0)
-    base = rng * BLOCK + sub * PIECE
-
-    def prepare(group, carry):
+    for group in range(SUBS):
         for h in range(2):
-            offset = params[group, 8 * h : 8 * h + 1, :]
-            sources = [jnp.clip(angle + offset + float(t - 1), 0.0, ANGLES - 1.0) for t in range(TAPS)]
-            weights = [params[group, 8 * h + 1 + t : 8 * h + 2 + t, :] for t in range(TAPS)]
-            for part in range(ANGLES // RADIX_B):
-                here = across + float(part * RADIX_B)
-                total = jnp.zeros((RADIX_B, ANGLES), F32)
-                for t in range(TAPS):
-                    total = total + jnp.where(here == sources[t], weights[t], 0.0)
-                band[2 * group + h, part * RADIX_B : (part + 1) * RADIX_B, :] = total.astype(BF16)
-            rate = params[group, 8 * h + 5 : 8 * h + 6, :]
-            by = jnp.broadcast_to(rate * (8.0 / SAMPLES), (8, ANGLES))
-            sr, si = jnp.cos(by), jnp.sin(by)
-            for stage in range(STAGES):
-                at = rate * ((base + stage * STAGE_BINS + row8).astype(F32) / SAMPLES)
-                pr, pi = jnp.cos(at), jnp.sin(at)
-                for t in range(PIECE // 8):
-                    part = slice(8 * t, 8 * t + 8)
-                    qr, qi = pr, pi
-                    for level in range(LEVELS):
-                        phase[stage * LEVELS + level, 2 * group + h, 0, part, :] = qr
-                        phase[stage * LEVELS + level, 2 * group + h, 1, part, :] = qi
-                        if level < LEVELS - 1:
-                            qr, qi = times(qr, qi, pr, pi)
-                    if t < PIECE // 8 - 1:
-                        pr, pi = times(pr, pi, sr, si)
+            rates[2 * group + h : 2 * group + h + 1, :] = params[group, 8 * h + 5 : 8 * h + 6, :]
+    base = (rng * BLOCK + sub * PIECE).astype(F32)
+    for n, bins in enumerate([base, 1.0, 2.0, 4.0, 8.0, float(STAGE_BINS)]):
+        at = rates[...] * (bins / SAMPLES)
+        turns[n, 0] = jnp.cos(at)
+        turns[n, 1] = jnp.sin(at)
+
+    def prepare(which, carry):
+        group, h = which // 2, lax.rem(which, 2)
+        own = params.at[group, pl.ds(pl.multiple_of(8 * h, 8), 8)]
+        sources = [jnp.clip(angle + own[0:1, :] + float(t - 1), 0.0, ANGLES - 1.0) for t in range(TAPS)]
+        weights = [own[1 + t : 2 + t, :] for t in range(TAPS)]
+
+        lower = angle < float(ANGLES // 2)
+        halved = [[jnp.where(lower == (block == 0), w, 0.0) for w in weights] for block in range(2)]
+
+        def fill(block, first, count, part):
+            lanes = slice(part * RADIX_B, (part + 1) * RADIX_B)
+            here = across[:count] + float(first)
+            total = jnp.zeros((count, RADIX_B), F32)
+            for t in range(TAPS):
+                total = total + jnp.where(here == sources[t][:, lanes], halved[block][t][:, lanes], 0.0)
+            row, col = first - block * RADIX_B, (part - block) * RADIX_B
+            band[which, block, row : row + count, col : col + RADIX_B] = total.astype(BF16)
+
+        fill(0, 0, 128, 0)
+        fill(0, 128, 16, 0)
+        fill(0, 112, 16, 1)
+        fill(0, 128, 80, 1)
+        fill(1, 176, 80, 1)
+        fill(1, 256, 16, 1)
+        fill(1, 240, 16, 2)
+        fill(1, 256, 128, 2)
+
+        def turn(n):
+            return tuple(turns[n, c, pl.ds(which, 1), :] for c in range(2))
+
+        def chosen(n, bit):
+            real, imag = turn(n)
+            on = lax.rem(row8 // bit, 2) == 1
+            return jnp.where(on, real, 1.0), jnp.where(on, imag, 0.0)
+
+        start = times(*times(*times(*chosen(1, 1), *chosen(2, 2)), *chosen(3, 4)), *turn(0))
+        by8, by_stage = turn(4), turn(5)
+        for stage in range(STAGES):
+            if stage:
+                start = times(*start, *by_stage)
+            at = start
+            for t in range(PIECE // 8):
+                part = slice(8 * t, 8 * t + 8)
+                now = at
+                for level in range(LEVELS):
+                    phase[stage * LEVELS + level, which, 0, part, :] = now[0]
+                    phase[stage * LEVELS + level, which, 1, part, :] = now[1]
+                    if level < LEVELS - 1:
+                        now = times(*now, *at)
+                if t < PIECE // 8 - 1:
+                    at = times(*at, *by8)
         return carry
 
-    lax.fori_loop(0, SUBS, prepare, 0)
+    lax.fori_loop(0, 2 * SUBS, prepare, 0)
 
     def image_copy(stage, src, dst, peer):
         return pltpu.make_async_remote_copy(
@@ -326,21 +365,24 @@
                 block = held[stage, :, c, row].reshape(PSUB, RADIX_B)
                 left[stage, row * RADIX_B : (row + 1) * RADIX_B, c * PSUB : (c + 1) * PSUB] = block.T
 
-        def make_image(k, carry):
+        parts = dot(left[stage], steer[...]).astype(BF16)
+        for c in range(2):
+            sent[stage, :, c] = parts[:, c * ANGLES : (c + 1) * ANGLES].reshape(SUBS, PIECE, ANGLES)
+
+        def send_image(k, carry):
             peer = lax.rem(sub + k, SUBS)
-            bins = pl.ds(pl.multiple_of(peer * PIECE, PIECE), PIECE)
-            part = dot(left[stage, bins, :], steer[...]).astype(BF16)
-            for c in range(2):
-                sent[stage, peer, c] = part[:, c * ANGLES : (c + 1) * ANGLES]
-
-            @pl.when(k < SUBS)
-            def _():
-                image_copy(stage, peer, sub, peer).start()
-
-            return carry
-
-        lax.fori_loop(1, SUBS + 1, make_image, 0)
+            image_copy(stage, peer, sub, peer).start()
+            return carry
+
+        lax.fori_loop(1, SUBS, send_image, 0)
         own_image(stage).start()
+
+    def resampled(values, which):
+        values = values.reshape(2 * PIECE, ANGLES)
+        low = dot(values[:, : 2 * RADIX_B], band[which, 0])
+        high = dot(values[:, RADIX_B:], band[which, 1])
+        middle = low[:, RADIX_B:] + high[:, :RADIX_B]
+        return jnp.concatenate([low[:, :RADIX_B], middle, high[:, RADIX_B:]], axis=1)
 
     def tile_copy(stage, src, dst, peer):
         return pltpu.make_async_remote_copy(
@@ -364,27 +406,35 @@
         own_image(stage).wait()
 
         def merge(i, carry):
-            level = i // SUBS
-            k = lax.rem(i, SUBS) + 1
-            group = lax.rem(sub + k, SUBS)
+            level = i // (SUBS // TOGETHER)
             now = lax.rem(level, 2)
             bit = 1 + level + level // 2
-            far_group = group + bit - 2 * bit * lax.rem(group // bit, 2)
             turn = phase.at[stage * LEVELS + level]
-            own = dot(image[stage, now, group].reshape(2 * PIECE, ANGLES), band[2 * group])
-            far = dot(image[stage, now, far_group].reshape(2 * PIECE, ANGLES), band[2 * group + 1])
-            ar, ai = times(own[:PIECE], own[PIECE:], turn[2 * group, 0], turn[2 * group, 1])
-            br, bi = times(far[:PIECE], far[PIECE:], turn[2 * group + 1, 0], turn[2 * group + 1, 1])
-            image[stage, 1 - now, group, 0] = (ar + br).astype(BF16)
-            image[stage, 1 - now, group, 1] = (ai + bi).astype(BF16)
-
-            @pl.when(jnp.logical_and(level == LEVELS - 1, k < SUBS))
+            last = lax.rem(i, SUBS // TOGETHER) * TOGETHER + 1
+            groups = [lax.rem(sub + last + j, SUBS) for j in range(TOGETHER)]
+            pairs = []
+            for group in groups:
+                far_group = group + bit - 2 * bit * lax.rem(group // bit, 2)
+                own = resampled(image[stage, now, group], 2 * group)
+                far = resampled(image[stage, now, far_group], 2 * group + 1)
+                pairs.append((own, far))
+            for group, (own, far) in zip(groups, pairs):
+                ar, ai = times(own[:PIECE], own[PIECE:], turn[2 * group, 0], turn[2 * group, 1])
+                br, bi = times(far[:PIECE], far[PIECE:], turn[2 * group + 1, 0], turn[2 * group + 1, 1])
+                image[stage, 1 - now, group, 0] = (ar + br).astype(BF16)
+                image[stage, 1 - now, group, 1] = (ai + bi).astype(BF16)
+
+            @pl.when(level == LEVELS - 1)
             def _():
-                tile_copy(stage, group, sub, group).start()
-
-            return carry
-
-        lax.fori_loop(0, LEVELS * SUBS, merge, 0)
+                for j, group in enumerate(groups):
+
+                    @pl.when(last + j < SUBS)
+                    def _():
+                        tile_copy(stage, group, sub, group).start()
+
+            return carry
+
+        lax.fori_loop(0, LEVELS * SUBS // TOGETHER, merge, 0)
         own_tile(stage).start()
 
     for stage in range(STAGES):
@@ -412,13 +462,11 @@
 def tile_kernel(x_ref, out_ref):
     for stage in range(STAGES):
         for c in range(2):
-            image = x_ref[stage, :, c].reshape(STAGE_BINS, ANGLES)
+            image = x_ref[stage, :, c].reshape(STAGE_BINS, RADIX_B)
             for row in range(STAGE_ROWS):
-                for part in range(ANGLES // RADIX_B):
-                    angles = slice(part * RADIX_B, (part + 1) * RADIX_B)
-                    start = stage * STAGE_BINS + row * RADIX_B
-                    values = image[row * RADIX_B : (row + 1) * RADIX_B, angles]
-                    out_ref[angles, c, start : start + RADIX_B] = values.astype(F32).T
+                start = stage * STAGE_BINS + row * RADIX_B
+                values = image[row * RADIX_B : (row + 1) * RADIX_B]
+                out_ref[:, c, start : start + RADIX_B] = values.T.astype(F32)
 
 
 def local(echoes, filter_spectrum, range_shifts, steering, tap_offsets, tap_weights, phase_rates):
@@ -450,13 +498,15 @@
             pltpu.VMEM((STAGES, RANKS, 2, STAGE_ROWS, PULSES, RADIX_B), BF16),
             pltpu.VMEM((STAGES, RANKS, 2, STAGE_ROWS, PULSES, RADIX_B), BF16),
             pltpu.VMEM((SUBS, PARAMS, ANGLES), F32),
+            pltpu.VMEM((2 * SUBS, ANGLES), F32),
+            pltpu.VMEM((6, 2, 2 * SUBS, ANGLES), F32),
             pltpu.VMEM((STAGES, STAGE_BINS, 2 * PSUB), BF16),
             pltpu.VMEM((2 * PSUB, 2 * ANGLES), BF16),
-            pltpu.VMEM((2 * SUBS, ANGLES, ANGLES), BF16),
+            pltpu.VMEM((2 * SUBS, 2, 2 * RADIX_B, 2 * RADIX_B), BF16),
             pltpu.VMEM((STAGES * LEVELS, 2 * SUBS, 2, PIECE, ANGLES), F32),
             pltpu.VMEM((STAGES, SUBS, 2, PIECE, ANGLES), BF16),
             pltpu.VMEM((STAGES, 2, SUBS, 2, PIECE, ANGLES), BF16),
-            dma((len(operands),)), dma((STEPS,)), dma((STAGES, RANKS)), dma((STAGES, RANKS)), dma((SUBS,)), dma((SUBS,)),
+            dma((len(operands),)), dma((ECHO_PARTS,)), dma((STAGES, RANKS)), dma((STAGES, RANKS)), dma((SUBS,)), dma((SUBS,)),
             dma((STAGES, SUBS)), dma((STAGES, SUBS)), dma((STAGES, SUBS)), dma((STAGES, SUBS)), dma((3 * STAGES,)),
         ],
         compiler_params=pltpu.CompilerParams(
@@ -464,13 +514,13 @@
         ),
         name="merge",
     )(*operands)
-    vmem = pl.BlockSpec(memory_space=pltpu.VMEM)
     return pl.pallas_call(
         tile_kernel,
         out_shape=jax.ShapeDtypeStruct((ANGLES, 2, BLOCK), F32),
-        in_specs=[vmem],
-        out_specs=vmem,
-        compiler_params=pltpu.CompilerParams(vmem_limit_bytes=32 << 20),
+        grid=(ANGLES // RADIX_B,),
+        in_specs=[pl.BlockSpec((STAGES, SUBS, 2, PIECE, RADIX_B), lambda i: (0, 0, 0, 0, i))],
+        out_specs=pl.BlockSpec((RADIX_B, 2, BLOCK), lambda i: (i, 0, 0)),
+        compiler_params=pltpu.CompilerParams(vmem_limit_bytes=56 << 20),
         name="tile",
     )(merged)
 

time: 67 us -> 60.2 us (0.90); the launches traced: 65.9 us -> 59.9 us
  Pallas kernels: 64.7 us -> 59.9 us
  local copies, waits for them, and re-layouts: 1.26 us -> 0 us
    pallas_call x1, Pallas kernels: 61.9 us -> 55.7 us  [local(): pl.pallas_call(kernel, out_shape=jax.ShapeDtypeStruct((STAGES, SUBS, 2, P...]
    pallas_call x1, Pallas kernels: 2.77 us -> 4.14 us  [local(): pl.pallas_call(tile_kernel, out_shape=jax.ShapeDtypeStruct((ANGLES, 2, BL...]
    unnamed x2 -> x0, local copies, waits for them, and re-layouts: 1.26 us -> none
where the time goes in v2:
time: 60.2 us; the launch traced here: 59.9 us
  Pallas kernels  59.9 us (100%)
    pallas_call x1, Pallas kernels, local(): pl.pallas_call(kernel, out_shape=jax.ShapeDtypeStruct((STAGES, SUBS, 2, P...  55.7 us
    pallas_call x1, Pallas kernels, local(): pl.pallas_call(tile_kernel, out_shape=jax.ShapeDtypeStruct((ANGLES, 2, BL...  4.14 us

profile of v2, /device:TPU:8, one launch (start us, length us, event | category | flops | bytes accessed | tf_op | source)
XLA Modules:
  0.0 59.9 jit_solution(13032905192524137215)
XLA Ops:
  0.0 55.7 %merge.1.x_ref = bf16[2,8,2,48,384]{4,3,2,1,0:T(8,128)(2,1)} custom-call(s32[256]{0:T(256)} %shift_hbm.1, f32[3072,128]{1,0:T(8,128)} %bitcast.14, f32[192,128]{1,0:T(8,128)} %bitcast.16, bf16[2,384,256]{2,1,0:T(8,128)(2,1)} %bitcast.15, s32[2,384]{1,0:T(2,128)} %bitcast.18, f32[2,4,384]{2,1,0:T(4,128)} %bitcast.17, f32[2,384]{1,0:T(2,128)} %bitcast.19, ...), custom_call_target="tpu_custom_call" | custom-call | tf_op jit(solution)/shard_map/merge/pallas_call | solution.py:489
  55.8 4.1 %tile.1 = f32[384,2,768]{2,1,0:T(2,128)} custom-call(bf16[2,8,2,48,384]{4,3,2,1,0:T(8,128)(2,1)} %merge.1.x_ref), custom_call_target="tpu_custom_call" | custom-call | tf_op jit(solution)/shard_map/tile/pallas_call | solution.py:517

commit v3 on v2

--- a/solution.py
+++ b/solution.py
@@ -24,11 +24,13 @@
 STAGE_ROWS = ROWS // STAGES
 STAGE_BINS = BLOCK // STAGES
 PIECE = STAGE_BINS // SUBS
-TOGETHER = 8
 ECHO_PARTS = 4
 HALO = 16
 LEVELS = 3
 PARAMS = 16
+IMAGE_ORDER = ((0, 1), (1, 0), (0, 3), (1, 2), (0, 2), (1, 1), (1, 3))
+TILE_ORDER = ((0, 1), (1, 0), (0, 3), (1, 2), (0, 2), (1, 1), (1, 3))
+TILE_ANGLES = 128
 MESH = pl.DeviceIdType.MESH
 F32 = jnp.float32
 BF16 = jnp.bfloat16
@@ -164,6 +166,13 @@
                 rows[pl.ds(start, RADIX_A, stride=PULSES), :] = values
 
 
+def nth_peer(index, size, k):
+    half = size // 2
+    across = (size - k) // half
+    step = lax.rem(k - across, half)
+    return lax.rem(index // half + across, 2) * half + lax.rem(lax.rem(index, half) + step, half)
+
+
 def kernel(
     shift_hbm, x_hbm, f_hbm, steer_hbm, off_hbm, weight_hbm, rate_hbm,
     wa_hbm, wb_hbm, vb_hbm, va_hbm, tw_hbm, back_hbm, lanes_hbm, out_ref,
@@ -234,7 +243,7 @@
     for stage in range(STAGES):
 
         def send_pulses(k, carry):
-            peer = lax.rem(rng + k, RANKS)
+            peer = nth_peer(rng, RANKS, k)
             pulse_copy(stage, peer, rng, peer).start()
             return carry
 
@@ -342,6 +351,9 @@
 
     lax.fori_loop(0, 2 * SUBS, prepare, 0)
 
+    def across(flip, step):
+        return lax.rem(sub // 4 + flip, 2) * 4 + lax.rem(lax.rem(sub, 4) + step, 4)
+
     def image_copy(stage, src, dst, peer):
         return pltpu.make_async_remote_copy(
             src_ref=sent.at[stage, src], dst_ref=image.at[stage, 0, dst], send_sem=image_send.at[stage, src],
@@ -369,12 +381,9 @@
         for c in range(2):
             sent[stage, :, c] = parts[:, c * ANGLES : (c + 1) * ANGLES].reshape(SUBS, PIECE, ANGLES)
 
-        def send_image(k, carry):
-            peer = lax.rem(sub + k, SUBS)
+        for flip, step in IMAGE_ORDER:
+            peer = across(flip, step)
             image_copy(stage, peer, sub, peer).start()
-            return carry
-
-        lax.fori_loop(1, SUBS, send_image, 0)
         own_image(stage).start()
 
     def resampled(values, which):
@@ -406,12 +415,11 @@
         own_image(stage).wait()
 
         def merge(i, carry):
-            level = i // (SUBS // TOGETHER)
+            level = i
             now = lax.rem(level, 2)
             bit = 1 + level + level // 2
             turn = phase.at[stage * LEVELS + level]
-            last = lax.rem(i, SUBS // TOGETHER) * TOGETHER + 1
-            groups = [lax.rem(sub + last + j, SUBS) for j in range(TOGETHER)]
+            groups = [across(flip, step) for flip, step in TILE_ORDER] + [sub]
             pairs = []
             for group in groups:
                 far_group = group + bit - 2 * bit * lax.rem(group // bit, 2)
@@ -426,15 +434,12 @@
 
             @pl.when(level == LEVELS - 1)
             def _():
-                for j, group in enumerate(groups):
-
-                    @pl.when(last + j < SUBS)
-                    def _():
-                        tile_copy(stage, group, sub, group).start()
+                for group in groups[:-1]:
+                    tile_copy(stage, group, sub, group).start()
 
             return carry
 
-        lax.fori_loop(0, LEVELS * SUBS // TOGETHER, merge, 0)
+        lax.fori_loop(0, LEVELS, merge, 0)
         own_tile(stage).start()
 
     for stage in range(STAGES):
@@ -459,14 +464,33 @@
         param_copy(sub, lax.rem(sub + k, SUBS)).wait_send()
 
 
-def tile_kernel(x_ref, out_ref):
-    for stage in range(STAGES):
-        for c in range(2):
-            image = x_ref[stage, :, c].reshape(STAGE_BINS, RADIX_B)
-            for row in range(STAGE_ROWS):
-                start = stage * STAGE_BINS + row * RADIX_B
-                values = image[row * RADIX_B : (row + 1) * RADIX_B]
-                out_ref[:, c, start : start + RADIX_B] = values.T.astype(F32)
+def tile_kernel(x_hbm, out_hbm, x_ref, out_ref, in_sem, out_sem):
+    def read(part):
+        lanes = slice(part * RADIX_B, (part + 1) * RADIX_B)
+        return pltpu.make_async_copy(x_hbm.at[:, :, :, :, lanes], x_ref.at[part], in_sem.at[part])
+
+    def write(n):
+        angles = pl.ds(n * TILE_ANGLES, TILE_ANGLES)
+        return pltpu.make_async_copy(out_ref.at[angles], out_hbm.at[angles], out_sem.at[n])
+
+    parts = ANGLES // RADIX_B
+    for part in range(parts):
+        read(part).start()
+    for part in range(parts):
+        read(part).wait()
+        for piece in range(RADIX_B // TILE_ANGLES):
+            lanes = slice(piece * TILE_ANGLES, (piece + 1) * TILE_ANGLES)
+            n = part * (RADIX_B // TILE_ANGLES) + piece
+            for stage in range(STAGES):
+                for c in range(2):
+                    image = x_ref[part, stage, :, c].reshape(STAGE_BINS, RADIX_B)
+                    for row in range(STAGE_ROWS):
+                        start = stage * STAGE_BINS + row * RADIX_B
+                        values = image[row * RADIX_B : (row + 1) * RADIX_B].T[lanes]
+                        out_ref[n * TILE_ANGLES : (n + 1) * TILE_ANGLES, c, start : start + RADIX_B] = values.astype(F32)
+            write(n).start()
+    for n in range(ANGLES // TILE_ANGLES):
+        write(n).wait()
 
 
 def local(echoes, filter_spectrum, range_shifts, steering, tap_offsets, tap_weights, phase_rates):
@@ -517,9 +541,14 @@
     return pl.pallas_call(
         tile_kernel,
         out_shape=jax.ShapeDtypeStruct((ANGLES, 2, BLOCK), F32),
-        grid=(ANGLES // RADIX_B,),
-        in_specs=[pl.BlockSpec((STAGES, SUBS, 2, PIECE, RADIX_B), lambda i: (0, 0, 0, 0, i))],
-        out_specs=pl.BlockSpec((RADIX_B, 2, BLOCK), lambda i: (i, 0, 0)),
+        in_specs=[hbm],
+        out_specs=hbm,
+        scratch_shapes=[
+            pltpu.VMEM((ANGLES // RADIX_B, STAGES, SUBS, 2, PIECE, RADIX_B), BF16),
+            pltpu.VMEM((ANGLES, 2, BLOCK), F32),
+            dma((ANGLES // RADIX_B,)),
+            dma((ANGLES // TILE_ANGLES,)),
+        ],
         compiler_params=pltpu.CompilerParams(vmem_limit_bytes=56 << 20),
         name="tile",
     )(merged)

time: 60.2 us -> 58.8 us (0.977)
  Pallas kernels: 59.9 us -> 58.5 us
    pallas_call x1, Pallas kernels: 4.14 us -> 3.38 us  [local(): pl.pallas_call(tile_kernel, out_shape=jax.ShapeDtypeStruct((ANGLES, 2, BL...]
    pallas_call x1, Pallas kernels: 55.7 us -> 55.1 us  [local(): pl.pallas_call(kernel, out_shape=jax.ShapeDtypeStruct((STAGES, SUBS, 2, P...]
where the time goes in v3:
time: 58.8 us; the launch traced here: 58.5 us
  Pallas kernels  58.5 us (99%)
    pallas_call x1, Pallas kernels, local(): pl.pallas_call(kernel, out_shape=jax.ShapeDtypeStruct((STAGES, SUBS, 2, P...  55.1 us
    pallas_call x1, Pallas kernels, local(): pl.pallas_call(tile_kernel, out_shape=jax.ShapeDtypeStruct((ANGLES, 2, BL...  3.38 us

profile of v3, /device:TPU:8, one launch (start us, length us, event | category | flops | bytes accessed | tf_op | source)
XLA Modules:
  0.0 58.5 jit_solution(17814450190423322438)
XLA Ops:
  0.0 55.1 %merge.1.x_hbm = bf16[2,8,2,48,384]{4,3,2,1,0:T(8,128)(2,1)} custom-call(s32[256]{0:T(256)} %shift_hbm.1, f32[3072,128]{1,0:T(8,128)} %bitcast.14, f32[192,128]{1,0:T(8,128)} %bitcast.16, bf16[2,384,256]{2,1,0:T(8,128)(2,1)} %bitcast.15, s32[2,384]{1,0:T(2,128)} %bitcast.18, f32[2,4,384]{2,1,0:T(4,128)} %bitcast.17, f32[2,384]{1,0:T(2,128)} %bitcast.19, ...), custom_call_target="tpu_custom_call" | custom-call | tf_op jit(solution)/shard_map/merge/pallas_call | solution.py:513
  55.1 3.4 %tile.1 = f32[384,2,768]{2,1,0:T(2,128)} custom-call(bf16[2,8,2,48,384]{4,3,2,1,0:T(8,128)(2,1)} %merge.1.x_hbm), custom_call_target="tpu_custom_call" | custom-call | tf_op jit(solution)/shard_map/tile/pallas_call | solution.py:541

commit v4 on v3

--- a/solution.py
+++ b/solution.py
@@ -28,6 +28,7 @@
 HALO = 16
 LEVELS = 3
 PARAMS = 16
+SPARE = 16
 IMAGE_ORDER = ((0, 1), (1, 0), (0, 3), (1, 2), (0, 2), (1, 1), (1, 3))
 TILE_ORDER = ((0, 1), (1, 0), (0, 3), (1, 2), (0, 2), (1, 1), (1, 3))
 TILE_ANGLES = 128
@@ -189,7 +190,7 @@
     for k in range(1, SUBS):
         pl.semaphore_signal(barrier, inc=1, device_id={"sub": lax.rem(sub + k, SUBS)}, device_id_type=MESH)
 
-    echo_rows = x_ref.shape[0] // ECHO_PARTS
+    echo_rows = x_hbm.shape[0] // ECHO_PARTS
 
     def echo_copy(i):
         part = pl.ds(i * echo_rows, echo_rows)
@@ -200,7 +201,7 @@
 
     names = ["wa", "tw", "wb", "filter", "shift", "lanes", "vb", "va", "back"]
     arrays = [
-        (wa_hbm, wa), (tw_hbm, tw), (wb_hbm, wb), (f_hbm, f_ref), (shift_hbm, shift_ref), (lanes_hbm, lanes),
+        (wa_hbm, wa), (tw_hbm, tw), (wb_hbm, wb), (f_hbm, f_ref.at[pl.ds(0, 2 * RADIX_A)]), (shift_hbm, shift_ref), (lanes_hbm, lanes),
         (vb_hbm, vb), (va_hbm, va), (back_hbm, back), (steer_hbm, steer_ref), (off_hbm, off_ref),
         (weight_hbm, weight_ref), (rate_hbm, rate_ref),
     ]
@@ -509,7 +510,11 @@
     ]
     hbm = pl.BlockSpec(memory_space=pltpu.HBM)
     dma = pltpu.SemaphoreType.DMA
-    landing = [pltpu.SMEM((PSUB,), jnp.int32)] + [pltpu.VMEM(x.shape, x.dtype) for x in operands[1:]]
+    landing = [
+        pltpu.SMEM((PSUB,), jnp.int32),
+        pltpu.VMEM((rows.shape[0] + SPARE, RADIX_B), F32),
+        pltpu.VMEM((filt.shape[0] + SPARE, RADIX_B), F32),
+    ] + [pltpu.VMEM(x.shape, x.dtype) for x in operands[3:]]
     merged = pl.pallas_call(
         kernel,
         out_shape=jax.ShapeDtypeStruct((STAGES, SUBS, 2, PIECE, ANGLES), BF16),
@@ -518,7 +523,7 @@
         scratch_shapes=[
             *landing,
             pltpu.VMEM((2, RADIX_A, RADIX_B), F32),
-            pltpu.VMEM((2 * RADIX_A * PULSES, RADIX_B), F32),
+            pltpu.VMEM((2 * RADIX_A * PULSES + SPARE, RADIX_B), F32),
             pltpu.VMEM((STAGES, RANKS, 2, STAGE_ROWS, PULSES, RADIX_B), BF16),
             pltpu.VMEM((STAGES, RANKS, 2, STAGE_ROWS, PULSES, RADIX_B), BF16),
             pltpu.VMEM((SUBS, PARAMS, ANGLES), F32),

time: 58.8 us -> 58.7 us (level)
  no operation moved by 1% of the time
where the time goes in v4:
time: 58.7 us; the launch traced here: 58.5 us
  Pallas kernels  58.5 us (100%)
    pallas_call x1, Pallas kernels, local(): pl.pallas_call(kernel, out_shape=jax.ShapeDtypeStruct((STAGES, SUBS, 2, P...  55.1 us
    pallas_call x1, Pallas kernels, local(): pl.pallas_call(tile_kernel, out_shape=jax.ShapeDtypeStruct((ANGLES, 2, BL...  3.38 us

profile of v4, /device:TPU:8, one launch (start us, length us, event | category | flops | bytes accessed | tf_op | source)
XLA Modules:
  0.0 58.5 jit_solution(16750764595055688289)
XLA Ops:
  0.0 55.1 %merge.1.x_hbm = bf16[2,8,2,48,384]{4,3,2,1,0:T(8,128)(2,1)} custom-call(s32[256]{0:T(256)} %shift_hbm.1, f32[3072,128]{1,0:T(8,128)} %bitcast.14, f32[192,128]{1,0:T(8,128)} %bitcast.16, bf16[2,384,256]{2,1,0:T(8,128)(2,1)} %bitcast.15, s32[2,384]{1,0:T(2,128)} %bitcast.18, f32[2,4,384]{2,1,0:T(4,128)} %bitcast.17, f32[2,384]{1,0:T(2,128)} %bitcast.19, ...), custom_call_target="tpu_custom_call" | custom-call | tf_op jit(solution)/shard_map/merge/pallas_call | solution.py:518
  55.1 3.4 %tile.1 = f32[384,2,768]{2,1,0:T(2,128)} custom-call(bf16[2,8,2,48,384]{4,3,2,1,0:T(8,128)(2,1)} %merge.1.x_hbm), custom_call_target="tpu_custom_call" | custom-call | tf_op jit(solution)/shard_map/tile/pallas_call | solution.py:546

commit v5 on v4

--- a/solution.py
+++ b/solution.py
@@ -24,14 +24,14 @@
 STAGE_ROWS = ROWS // STAGES
 STAGE_BINS = BLOCK // STAGES
 PIECE = STAGE_BINS // SUBS
-ECHO_PARTS = 4
+ECHO_PARTS = 8
 HALO = 16
 LEVELS = 3
 PARAMS = 16
 SPARE = 16
 IMAGE_ORDER = ((0, 1), (1, 0), (0, 3), (1, 2), (0, 2), (1, 1), (1, 3))
 TILE_ORDER = ((0, 1), (1, 0), (0, 3), (1, 2), (0, 2), (1, 1), (1, 3))
-TILE_ANGLES = 128
+TILE_ANGLES = 64
 MESH = pl.DeviceIdType.MESH
 F32 = jnp.float32
 BF16 = jnp.bfloat16
@@ -114,8 +114,7 @@
     arrived("wa")
     arrived("tw")
     for j in pairs:
-        if j % 2 == 0:
-            arrived(j // 2)
+        arrived(j)
         signal = []
         for q in range(2):
             start = pulse[j][q] * 2 * RADIX_A
@@ -209,7 +208,7 @@
     late_loads = copies[len(names) :]
     loads = dict(zip(names, copies))
     loads.update({i: echo_copy(i) for i in range(ECHO_PARTS)})
-    order = ["wa", 0, "tw", 1, "wb", 2, 3, "filter", "shift", "lanes", "vb", "va", "back"]
+    order = [0, "wa", 1, "tw", 2, 3, "wb", 4, 5, 6, 7, "filter", "shift", "lanes", "vb", "va", "back"]
     for name in order:
         loads[name].start()
     for copy in late_loads:
@@ -466,9 +465,11 @@
 
 
 def tile_kernel(x_hbm, out_hbm, x_ref, out_ref, in_sem, out_sem):
-    def read(part):
+    def read(part, stage):
         lanes = slice(part * RADIX_B, (part + 1) * RADIX_B)
-        return pltpu.make_async_copy(x_hbm.at[:, :, :, :, lanes], x_ref.at[part], in_sem.at[part])
+        return pltpu.make_async_copy(
+            x_hbm.at[stage, :, :, :, lanes], x_ref.at[part, stage], in_sem.at[part, stage]
+        )
 
     def write(n):
         angles = pl.ds(n * TILE_ANGLES, TILE_ANGLES)
@@ -476,13 +477,15 @@
 
     parts = ANGLES // RADIX_B
     for part in range(parts):
-        read(part).start()
+        for stage in range(STAGES):
+            read(part, stage).start()
     for part in range(parts):
-        read(part).wait()
         for piece in range(RADIX_B // TILE_ANGLES):
             lanes = slice(piece * TILE_ANGLES, (piece + 1) * TILE_ANGLES)
             n = part * (RADIX_B // TILE_ANGLES) + piece
             for stage in range(STAGES):
+                if piece == 0:
+                    read(part, stage).wait()
                 for c in range(2):
                     image = x_ref[part, stage, :, c].reshape(STAGE_BINS, RADIX_B)
                     for row in range(STAGE_ROWS):
@@ -551,7 +554,7 @@
         scratch_shapes=[
             pltpu.VMEM((ANGLES // RADIX_B, STAGES, SUBS, 2, PIECE, RADIX_B), BF16),
             pltpu.VMEM((ANGLES, 2, BLOCK), F32),
-            dma((ANGLES // RADIX_B,)),
+            dma((ANGLES // RADIX_B, STAGES)),
             dma((ANGLES // TILE_ANGLES,)),
         ],
         compiler_params=pltpu.CompilerParams(vmem_limit_bytes=56 << 20),

time: 58.7 us -> 58.6 us (level)
  no operation moved by 1% of the time
where the time goes in v5:
time: 58.6 us; the launch traced here: 58.4 us
  Pallas kernels  58.4 us (100%)
    pallas_call x1, Pallas kernels, local(): pl.pallas_call(kernel, out_shape=jax.ShapeDtypeStruct((STAGES, SUBS, 2, P...  55 us
    pallas_call x1, Pallas kernels, local(): pl.pallas_call(tile_kernel, out_shape=jax.ShapeDtypeStruct((ANGLES, 2, BL...  3.41 us

profile of v5, /device:TPU:8, one launch (start us, length us, event | category | flops | bytes accessed | tf_op | source)
XLA Modules:
  0.0 58.4 jit_solution(15992311103884367642)
XLA Ops:
  0.0 55.0 %merge.1.x_hbm = bf16[2,8,2,48,384]{4,3,2,1,0:T(8,128)(2,1)} custom-call(s32[256]{0:T(256)} %shift_hbm.1, f32[3072,128]{1,0:T(8,128)} %bitcast.14, f32[192,128]{1,0:T(8,128)} %bitcast.16, bf16[2,384,256]{2,1,0:T(8,128)(2,1)} %bitcast.15, s32[2,384]{1,0:T(2,128)} %bitcast.18, f32[2,4,384]{2,1,0:T(4,128)} %bitcast.17, f32[2,384]{1,0:T(2,128)} %bitcast.19, ...), custom_call_target="tpu_custom_call" | custom-call | tf_op jit(solution)/shard_map/merge/pallas_call | solution.py:521
  55.0 3.4 %tile.1 = f32[384,2,768]{2,1,0:T(2,128)} custom-call(bf16[2,8,2,48,384]{4,3,2,1,0:T(8,128)(2,1)} %merge.1.x_hbm), custom_call_target="tpu_custom_call" | custom-call | tf_op jit(solution)/shard_map/tile/pallas_call | solution.py:549

commit v6 on v5

--- a/solution.py
+++ b/solution.py
@@ -240,22 +240,6 @@
     def own_pulses(stage):
         return pltpu.make_async_copy(pulses.at[stage, rng], held.at[stage, rng], local_sem.at[stage])
 
-    for stage in range(STAGES):
-
-        def send_pulses(k, carry):
-            peer = nth_peer(rng, RANKS, k)
-            pulse_copy(stage, peer, rng, peer).start()
-            return carry
-
-        lax.fori_loop(1, RANKS, send_pulses, 0)
-        own_pulses(stage).start()
-
-    def clear(which, carry):
-        band[which] = jnp.zeros((2, 2 * RADIX_B, 2 * RADIX_B), BF16)
-        return carry
-
-    lax.fori_loop(0, 2 * SUBS, clear, 0)
-
     for copy in late_loads:
         copy.wait()
     for h in range(2):
@@ -272,6 +256,22 @@
 
     for k in range(1, SUBS):
         param_copy(sub, lax.rem(sub + k, SUBS)).start()
+
+    for stage in range(STAGES):
+
+        def send_pulses(k, carry):
+            peer = nth_peer(rng, RANKS, k)
+            pulse_copy(stage, peer, rng, peer).start()
+            return carry
+
+        lax.fori_loop(1, RANKS, send_pulses, 0)
+        own_pulses(stage).start()
+
+    def clear(which, carry):
+        band[which] = jnp.zeros((2, 2 * RADIX_B, 2 * RADIX_B), BF16)
+        return carry
+
+    lax.fori_loop(0, 2 * SUBS, clear, 0)
 
     real = steer_ref[0].astype(F32)
     imag = steer_ref[1].astype(F32)

time: 58.6 us -> 57.9 us (0.988)
  the two profiles are of different devices: /device:TPU:8 before, /device:TPU:1 now
where the time goes in v6:
time: 57.9 us; the launch traced here: 57.8 us
  Pallas kernels  57.8 us (100%)
    pallas_call x1, Pallas kernels, local(): pl.pallas_call(kernel, out_shape=jax.ShapeDtypeStruct((STAGES, SUBS, 2, P...  54.4 us
    pallas_call x1, Pallas kernels, local(): pl.pallas_call(tile_kernel, out_shape=jax.ShapeDtypeStruct((ANGLES, 2, BL...  3.41 us

profile of v6, /device:TPU:1, one launch (start us, length us, event | category | flops | bytes accessed | tf_op | source)
XLA Modules:
  0.0 57.8 jit_solution(2088786282922183060)
XLA Ops:
  0.0 54.4 %merge.1.x_hbm = bf16[2,8,2,48,384]{4,3,2,1,0:T(8,128)(2,1)} custom-call(s32[256]{0:T(256)} %shift_hbm.1, f32[3072,128]{1,0:T(8,128)} %bitcast.14, f32[192,128]{1,0:T(8,128)} %bitcast.16, bf16[2,384,256]{2,1,0:T(8,128)(2,1)} %bitcast.15, s32[2,384]{1,0:T(2,128)} %bitcast.18, f32[2,4,384]{2,1,0:T(4,128)} %bitcast.17, f32[2,384]{1,0:T(2,128)} %bitcast.19, ...), custom_call_target="tpu_custom_call" | custom-call | tf_op jit(solution)/shard_map/merge/pallas_call | solution.py:521
  54.4 3.4 %tile.1 = f32[384,2,768]{2,1,0:T(2,128)} custom-call(bf16[2,8,2,48,384]{4,3,2,1,0:T(8,128)(2,1)} %merge.1.x_hbm), custom_call_target="tpu_custom_call" | custom-call | tf_op jit(solution)/shard_map/tile/pallas_call | solution.py:549
